TPU v7x, 32 devices: a whole 2x2x4 slice. The times are simulated.
32 devices in a mesh: ckpt: 4 (over y, x), vocab: 8 (over z, core).
Axes of the slice: x: 2, y: 2, z: 4, core: 2. Of those that a mesh axis runs over, the one named last changes fastest.
Arguments:
- token_ids: int32 [1024], P('vocab'), may hold values from 0 to 1023, as said below
- grad_values: bfloat16 [4, 1024, 8192], P('ckpt', 'vocab'), may hold values from -6 to 6
- grad_scales: float32 [4, 64, 1024], P('ckpt', None, 'vocab'), may hold values from 0.3 to 3
- tables: bfloat16 [4, 1024, 8192], P('ckpt', 'vocab'), may hold values from -6 to 6
Outputs:
- merged: bfloat16 [1024, 8192], P('vocab', 'ckpt')
Inputs may be any that keep to these rules, and one draw needn't show every extreme that they name: The owner of a token is token_ids // 128. Among the 128 tokens of each index of vocab, exactly 4 owners appear, each with exactly 32 tokens; one owner appears in every index's tokens. Ids repeat and some owners are far more frequent than others.
All inputs are finite; a program needn't handle non-finite values.
Results may differ from a plain program's by a relative error of at most 0.018.
Values may be sent and summed in bfloat16 or wider, within the bound.
A program may use at most 64 MiB of HBM per device.

v0:
```python
import functools

import jax
import jax.numpy as jnp
from jax import lax
from jax.experimental import pallas as pl
from jax.experimental.pallas import tpu as pltpu
from jax.sharding import PartitionSpec as P

BLK = 128
CHUNKS = 16
CHAIN_CHUNKS = 32
LAG = 4
SETTLE = 2
LOADS = (8, 9, 10, 11, 12)
MESH = pl.DeviceIdType.MESH


prior_weight = 1.0


def merge_kernel(
    groups,
    ckpts,
    chunks,
    ids_ref,
    grads_ref,
    all_scales_ref,
    tables_ref,
    out_ref,
    grads,
    tables,
    scales_ref,
    match_ref,
    select_ref,
    tag_send,
    tag_recv,
    send,
    recv,
    part_send,
    part_recv,
    load_sem,
    tag_send_sem,
    tag_recv_sem,
    send_sem,
    recv_sem,
    part_send_sem,
    part_recv_sem,
):
    c = lax.axis_index("ckpt")
    v = lax.axis_index("vocab")
    rows = tables.shape[0]
    count = grads.shape[0]
    width = grads.shape[1]
    slots = match_ref.shape[0]
    capacity = slots // groups
    quarter = width // ckpts
    piece = quarter // chunks
    blocks = piece // BLK

    def vocab_peer(j):
        return (c, lax.rem(v + j, groups))

    def ckpt_peer(j):
        return (lax.rem(c + j, ckpts), v)

    barrier = pltpu.get_barrier_semaphore()
    for j in range(1, groups):
        pl.semaphore_signal(barrier, inc=1, device_id=vocab_peer(j), device_id_type=MESH)
    for j in range(1, ckpts):
        pl.semaphore_signal(barrier, inc=1, device_id=ckpt_peer(j), device_id_type=MESH)

    load_grads = pltpu.make_async_copy(grads_ref, grads, load_sem.at[0])
    load_tables = pltpu.make_async_copy(tables_ref, tables, load_sem.at[1])
    load_scales = pltpu.make_async_copy(all_scales_ref, scales_ref, load_sem.at[2])
    load_grads.start()
    load_scales.start()
    load_tables.start()

    ids_row = ids_ref[...]
    ids_col = jnp.broadcast_to(ids_row, (count, count)).T
    near_row = lax.rem(ids_row // rows - v + groups, groups)
    near_col = lax.rem(ids_col // rows - v + groups, groups)
    same = near_row == near_col
    at0 = lax.broadcasted_iota(jnp.int32, (count, count), 0)
    at1 = lax.broadcasted_iota(jnp.int32, (count, count), 1)
    rank_row = jnp.sum(jnp.where(same & (at0 < at1), 1, 0), axis=0, keepdims=True)
    rank_col = jnp.sum(jnp.where(same & (at1 < at0), 1, 0), axis=1, keepdims=True)
    slot_row = near_row * capacity + rank_row
    slot_col = near_col * capacity + rank_col
    match_ref[...] = jnp.where(
        lax.broadcasted_iota(jnp.int32, (slots, count), 0) == slot_row, 1.0, 0.0
    ).astype(jnp.bfloat16)
    tags = jnp.sum(
        jnp.where(
            lax.broadcasted_iota(jnp.int32, (count, slots), 1) == slot_col[:, 0:1],
            lax.rem(ids_col[:, 0:1], rows),
            0,
        ),
        axis=0,
        keepdims=True,
    )
    tag_send[...] = jnp.broadcast_to(tags, tag_send.shape)

    def tag_copy(j):
        return pltpu.make_async_remote_copy(
            src_ref=tag_send,
            dst_ref=tag_recv.at[j],
            send_sem=tag_send_sem.at[j],
            recv_sem=tag_recv_sem.at[j],
            device_id=vocab_peer(j),
            device_id_type=MESH,
        )

    def row_copy(k, j):
        return pltpu.make_async_remote_copy(
            src_ref=send.at[k, j],
            dst_ref=recv.at[k, j],
            send_sem=send_sem.at[k, j],
            recv_sem=recv_sem.at[k, j],
            device_id=vocab_peer(j),
            device_id_type=MESH,
        )

    def part_copy(k, j):
        return pltpu.make_async_remote_copy(
            src_ref=part_send.at[k, j],
            dst_ref=part_recv.at[k, j],
            send_sem=part_send_sem.at[k, j],
            recv_sem=part_recv_sem.at[k, j],
            device_id=ckpt_peer(j),
            device_id_type=MESH,
        )

    order = sorted(range(1, groups), key=lambda j: -min(j, groups - j))

    def place(k):
        block_scales = jnp.concatenate(
            [
                scales_ref[pl.ds(q * (quarter // BLK) + k * blocks, blocks), :]
                for q in range(ckpts)
            ],
            axis=0,
        ).T
        squares = []
        for q in range(ckpts):
            for b in range(blocks):
                at = pl.multiple_of(q * quarter + k * piece + b * BLK, BLK)
                i = q * blocks + b
                g = grads[:, pl.ds(at, BLK)].astype(jnp.float32) * block_scales[:, i : i + 1]
                squares.append((g * g).astype(jnp.bfloat16))
        placed = jnp.dot(
            match_ref[...],
            jnp.concatenate(squares, axis=1),
            preferred_element_type=jnp.float32,
        ).astype(jnp.bfloat16)
        placed = placed.reshape(groups, capacity, ckpts * piece)
        recv[k, 0] = placed[0]
        for j in range(1, groups):
            send[k, j] = placed[j]

    def start_rows(k):
        for j in order:
            row_copy(k, j).start()

    load_grads.wait()
    load_scales.wait()
    place(0)
    pl.semaphore_wait(barrier, groups + ckpts - 2)
    for j in order:
        tag_copy(j).start()
    start_rows(0)

    def place_next(k, carry):
        place(k)
        start_rows(k)
        return carry

    lax.fori_loop(1, chunks, place_next, 0)

    lane = lax.broadcasted_iota(jnp.int32, (1, slots), 1) // capacity
    arrived_tags = jnp.where(lane == 0, tags, 0)
    for j in range(1, groups):
        tag_copy(j).wait()
        arrived_tags = jnp.where(lane == j, tag_recv[j, 0:1, :], arrived_tags)
    select_ref[...] = jnp.where(
        lax.broadcasted_iota(jnp.int32, (rows, slots), 0) == arrived_tags, 1.0, 0.0
    ).astype(jnp.bfloat16)
    load_tables.wait()

    def weigh_chunk(k):
        for j in range(1, groups):
            row_copy(k, j).wait_recv()
        fisher = jnp.dot(
            select_ref[...],
            recv[k].reshape(slots, ckpts * piece),
            preferred_element_type=jnp.float32,
        )
        weight = (fisher + prior_weight).astype(jnp.bfloat16)
        for q in range(ckpts):
            own = weight[:, q * piece : (q + 1) * piece]
            at = pl.multiple_of(q * quarter + k * piece, BLK)
            table = tables[:, pl.ds(at, piece)].astype(jnp.float32)
            j = lax.rem(q - c + ckpts, ckpts)
            part_send[k, j, 0] = (own.astype(jnp.float32) * table).astype(jnp.bfloat16)
            part_send[k, j, 1] = own
        for j in range(1, ckpts):
            part_copy(k, j).start()

    def finish_chunk(k):
        numer = part_send[k, 0, 0].astype(jnp.float32)
        denom = part_send[k, 0, 1].astype(jnp.float32)
        for j in range(1, ckpts):
            part_copy(k, j).wait_recv()
            numer += part_recv[k, j, 0].astype(jnp.float32)
            denom += part_recv[k, j, 1].astype(jnp.float32)
        at = pl.multiple_of(k * piece, BLK)
        out_ref[:, pl.ds(at, piece)] = (numer / denom).astype(jnp.bfloat16)

    weigh_chunk(0)

    def step(k, carry):
        weigh_chunk(k)
        finish_chunk(k - 1)
        return carry

    lax.fori_loop(1, chunks, step, 0)
    finish_chunk(chunks - 1)

    def drain(k, carry):
        for j in range(1, groups):
            row_copy(k, j).wait_send()
        for j in range(1, ckpts):
            part_copy(k, j).wait_send()
        return carry

    lax.fori_loop(0, chunks, drain, 0)


def merge_rows(token_ids, grad_values, grad_scales, tables):
    groups = lax.axis_size("vocab")
    ckpts = lax.axis_size("ckpt")
    rows, width = tables.shape[1:]
    count = token_ids.shape[0]
    slots = 2 * count
    capacity = slots // groups
    chunk_width = width // CHUNKS
    vmem = pl.BlockSpec(memory_space=pltpu.VMEM)
    hbm = pl.BlockSpec(memory_space=pl.ANY)
    bf16 = jnp.bfloat16
    dma = pltpu.SemaphoreType.DMA
    return pl.pallas_call(
        functools.partial(merge_kernel, groups, ckpts, CHUNKS),
        out_shape=jax.ShapeDtypeStruct((rows, width // ckpts), bf16),
        in_specs=[vmem, hbm, hbm, hbm],
        out_specs=vmem,
        scratch_shapes=[
            pltpu.VMEM((count, width), bf16),
            pltpu.VMEM((rows, width), bf16),
            pltpu.VMEM((width // BLK, count), jnp.float32),
            pltpu.VMEM((slots, count), bf16),
            pltpu.VMEM((rows, slots), bf16),
            pltpu.VMEM((8, slots), jnp.int32),
            pltpu.VMEM((groups, 8, slots), jnp.int32),
            pltpu.VMEM((CHUNKS, groups, capacity, chunk_width), bf16),
            pltpu.VMEM((CHUNKS, groups, capacity, chunk_width), bf16),
            pltpu.VMEM((CHUNKS, ckpts, 2, rows, chunk_width // ckpts), bf16),
            pltpu.VMEM((CHUNKS, ckpts, 2, rows, chunk_width // ckpts), bf16),
            dma((3,)),
            dma((groups,)),
            dma((groups,)),
            dma((CHUNKS, groups)),
            dma((CHUNKS, groups)),
            dma((CHUNKS, ckpts)),
            dma((CHUNKS, ckpts)),
        ],
        compiler_params=pltpu.CompilerParams(
            collective_id=9, has_side_effects=True, vmem_limit_bytes=60 * 1024 * 1024
        ),
        cost_estimate=pl.CostEstimate(
            flops=4 * slots * count * width,
            bytes_accessed=5 * rows * width,
            transcendentals=0,
        ),
    )(
        token_ids.reshape(1, count),
        grad_values[0],
        grad_scales[0],
        tables[0],
    )


def sort_positions(ids_row, rows):
    count = ids_row.shape[1]
    ids_col = jnp.broadcast_to(ids_row, (count, count)).T
    own_row = ids_row // rows
    own_col = ids_col // rows
    at0 = lax.broadcasted_iota(jnp.int32, (count, count), 0)
    at1 = lax.broadcasted_iota(jnp.int32, (count, count), 1)
    same = own_row == own_col
    first0 = (own_col < own_row) | (same & (at0 < at1))
    first1 = (own_row < own_col) | (same & (at1 < at0))
    pos_row = jnp.sum(jnp.where(first0, 1, 0), axis=0, keepdims=True)
    pos_col = jnp.sum(jnp.where(first1, 1, 0), axis=1, keepdims=True)
    return pos_row, pos_col, ids_col[:, 0:1]


def gather_kernel(groups, rows, capacity, ids_ref, ids_out, branch_out, mine, theirs, send_sem, recv_sem):
    c = lax.axis_index("ckpt")
    v = lax.axis_index("vocab")
    count = ids_ref.shape[1]

    def peer(j):
        return (c, lax.rem(v + j, groups))

    barrier = pltpu.get_barrier_semaphore()
    for j in range(1, groups):
        pl.semaphore_signal(barrier, inc=1, device_id=peer(j), device_id_type=MESH)
    _, pos_col, ids_col = sort_positions(ids_ref[...], rows)
    at1 = lax.broadcasted_iota(jnp.int32, (count, count), 1)
    ordered = jnp.sum(jnp.where(at1 == pos_col, ids_col, 0), axis=0, keepdims=True)
    mine[...] = jnp.broadcast_to(ordered, mine.shape)
    theirs[v] = mine[...]

    def copy(j):
        return pltpu.make_async_remote_copy(
            src_ref=mine,
            dst_ref=theirs.at[v],
            send_sem=send_sem.at[j],
            recv_sem=recv_sem.at[j],
            device_id=peer(j),
            device_id_type=MESH,
        )

    pl.semaphore_wait(barrier, groups - 1)
    for j in range(1, groups):
        copy(j).start()
    for j in range(1, groups):
        copy(j).wait()
    ids_all = jnp.concatenate([theirs[d, 0:1, :] for d in range(groups)], axis=0)
    ids_out[...] = ids_all
    layer = lax.broadcasted_iota(jnp.int32, (groups, count), 0) // 2
    owner_layer = ids_all // (2 * rows)
    most = jnp.zeros((1, 1), jnp.int32)
    for cut in range(groups // 2 - 1):
        up = jnp.where((layer <= cut) & (owner_layer > cut), 1, 0)
        down = jnp.where((layer > cut) & (owner_layer <= cut), 1, 0)
        for flow in (up, down):
            total = jnp.sum(jnp.sum(flow, axis=1, keepdims=True), axis=0, keepdims=True)
            most = jnp.maximum(most, total)
    most = jnp.max(most)
    branch_out[0] = sum(jnp.where(most > load * capacity, 1, 0) for load in LOADS)


def chain_kernel(
    groups,
    ckpts,
    chunks,
    span,
    ids_ref,
    ids_all_ref,
    grads_ref,
    all_scales_ref,
    tables_ref,
    out_ref,
    grads,
    tables,
    scales_ref,
    match_ref,
    up_pool_sel,
    up_in_sel,
    down_pool_sel,
    down_in_sel,
    rows_pool_sel,
    rows_up_sel,
    rows_down_sel,
    pool,
    up_in,
    down_in,
    up_out,
    down_out,
    part,
    part_x,
    sum_send,
    sum_recv,
    load_sem,
    pool_sems,
    up_sems,
    up_mate_sems,
    down_sems,
    down_mate_sems,
    x_sems,
    y_sems,
):
    c = lax.axis_index("ckpt")
    v = lax.axis_index("vocab")
    layers = groups // 2
    z = v // 2
    core = v % 2
    mate = v + 1 - 2 * core
    rows = tables.shape[0]
    count = grads.shape[0]
    width = grads.shape[1]
    quarter = width // ckpts
    piece = 2 * quarter // chunks
    blocks = piece // BLK
    bf16 = jnp.bfloat16
    has_up = z < layers - 1
    has_down = z > 0

    y, x = c // 2, c % 2
    x_peer = (y * 2 + 1 - x, v)
    y_peer = ((1 - y) * 2 + x, v)

    def greet(device):
        pl.semaphore_signal(barrier, inc=1, device_id=device, device_id_type=MESH)

    barrier = pltpu.get_barrier_semaphore()
    greet((c, mate))
    greet(x_peer)
    greet(y_peer)

    @pl.when(has_up)
    def _():
        greet((c, v + 2))

    @pl.when(has_down)
    def _():
        greet((c, v - 2))

    load_grads = pltpu.make_async_copy(grads_ref, grads, load_sem.at[0])
    load_tables = pltpu.make_async_copy(tables_ref, tables, load_sem.at[1])
    load_scales = pltpu.make_async_copy(all_scales_ref, scales_ref, load_sem.at[2])
    load_grads.start()
    load_scales.start()
    load_tables.start()

    pos_row, _, _ = sort_positions(ids_ref[...], rows)
    at0 = lax.broadcasted_iota(jnp.int32, (count, count), 0)
    at1 = lax.broadcasted_iota(jnp.int32, (count, count), 1)
    match_ref[...] = jnp.where(at0 == pos_row, 1.0, 0.0).astype(bf16)

    ids_all = ids_all_ref[...]
    layer = lax.broadcasted_iota(jnp.int32, (groups, count), 0) // 2
    owner_layer = ids_all // (2 * rows)
    before = jnp.where(at0 < at1, 1.0, 0.0).astype(bf16)

    def places(mask):
        flags = jnp.where(mask, 1.0, 0.0)
        inner = jnp.dot(flags.astype(bf16), before, preferred_element_type=jnp.float32)
        totals = jnp.sum(flags, axis=1, keepdims=True)
        offset = jnp.zeros((1, 1), jnp.float32)
        offsets = []
        for d in range(groups):
            offsets.append(offset)
            offset = offset + totals[d : d + 1]
        place = (inner + jnp.concatenate(offsets, axis=0)).astype(jnp.int32)
        return jnp.where(mask, place, -1)

    up_from = places((layer <= z - 1) & (owner_layer > z - 1))
    up_to = places((layer <= z) & (owner_layer > z))
    down_from = places((layer >= z + 1) & (owner_layer < z + 1))
    down_to = places((layer >= z) & (owner_layer < z))

    def one_hot(size, values):
        shape = (size, count)
        return jnp.where(
            lax.broadcasted_iota(jnp.int32, shape, 0) == values, 1.0, 0.0
        ).astype(bf16)

    def meet(a, b):
        return lax.dot_general(
            a, b, (((1,), (1,)), ((), ())), preferred_element_type=jnp.float32
        )

    up_sum = down_sum = rows_up = rows_down = 0.0
    pools = [[0.0, 0.0] for _ in range(3)]
    for d in range(groups):
        take_up = one_hot(span, up_to[d : d + 1] - core * span)
        take_down = one_hot(span, down_to[d : d + 1] - core * span)
        take_rows = one_hot(rows, ids_all[d : d + 1] - v * rows)
        at_up = one_hot(2 * span, up_from[d : d + 1])
        at_down = one_hot(2 * span, down_from[d : d + 1])
        up_sum += meet(take_up, at_up)
        down_sum += meet(take_down, at_down)
        rows_up += meet(take_rows, at_up)
        rows_down += meet(take_rows, at_down)
        here = jnp.where(z == d // 2, 1.0, 0.0).astype(bf16)
        for i, take in enumerate((take_up, take_down, take_rows)):
            pools[i][d % 2] += take * here
    up_in_sel[...] = up_sum.astype(bf16)
    down_in_sel[...] = down_sum.astype(bf16)
    rows_up_sel[...] = rows_up.astype(bf16)
    rows_down_sel[...] = rows_down.astype(bf16)
    for ref, pair in zip((up_pool_sel, down_pool_sel, rows_pool_sel), pools):
        ref[...] = jnp.concatenate(pair, axis=1).astype(bf16)

    @pl.when(z == 0)
    def _():
        def clear(k, carry):
            up_in[k] = jnp.zeros(up_in.shape[1:], bf16)
            return carry

        lax.fori_loop(0, chunks, clear, 0)

    @pl.when(z == layers - 1)
    def _():
        def clear(k, carry):
            down_in[k] = jnp.zeros(down_in.shape[1:], bf16)
            return carry

        lax.fori_loop(0, chunks, clear, 0)

    def remote(src, dst, sems, k, device):
        return pltpu.make_async_remote_copy(
            src_ref=src,
            dst_ref=dst,
            send_sem=sems.at[0, k],
            recv_sem=sems.at[1, k],
            device_id=device,
            device_id_type=MESH,
        )

    def pool_copy(k):
        return remote(pool.at[k, core], pool.at[k, core], pool_sems, k, (c, mate))

    def up_copy(k):
        return remote(up_out.at[k], up_in.at[k, core], up_sems, k, (c, lax.rem(v + 2, groups)))

    def down_copy(k):
        device = (c, lax.rem(v + groups - 2, groups))
        return remote(down_out.at[k], down_in.at[k, core], down_sems, k, device)

    def up_mate(k):
        return remote(up_in.at[k, core], up_in.at[k, core], up_mate_sems, k, (c, mate))

    def down_mate(k):
        return remote(down_in.at[k, core], down_in.at[k, core], down_mate_sems, k, (c, mate))

    def x_copy(k):
        return remote(part.at[k], part_x.at[k], x_sems, k, x_peer)

    def y_copy(k):
        return remote(sum_send.at[k], sum_recv.at[k], y_sems, k, y_peer)

    def column(k, i):
        return (i * 2 + k % 2) * quarter + (k // 2) * piece

    def place(k):
        block_scales = jnp.concatenate(
            [
                scales_ref[pl.ds(pl.multiple_of(column(k, i) // BLK, blocks), blocks), :]
                for i in range(2)
            ],
            axis=0,
        ).T
        squares = []
        for i in range(2):
            for b in range(blocks):
                at = pl.multiple_of(column(k, i) + b * BLK, BLK)
                n = i * blocks + b
                g = grads[:, pl.ds(at, BLK)].astype(jnp.float32) * block_scales[:, n : n + 1]
                squares.append((g * g).astype(bf16))
        pool[k, core] = jnp.dot(
            match_ref[...],
            jnp.concatenate(squares, axis=1),
            preferred_element_type=jnp.float32,
        ).astype(bf16)

    def pooled(k):
        return pool[k].reshape(2 * count, 2 * piece)

    def arrived(ref, k):
        return ref[k].reshape(2 * span, 2 * piece)

    def dot(a, b):
        return jnp.dot(a, b, preferred_element_type=jnp.float32)

    def weigh_chunk(k):
        fisher = (
            dot(rows_pool_sel[...], pooled(k))
            + dot(rows_up_sel[...], arrived(up_in, k))
            + dot(rows_down_sel[...], arrived(down_in, k))
        )
        weight = (fisher + prior_weight).astype(bf16)
        for i in range(2):
            own = weight[:, i * piece : (i + 1) * piece]
            at = pl.multiple_of(column(k, i), BLK)
            table = tables[:, pl.ds(at, piece)].astype(jnp.float32)
            to_y = (i + y) % 2
            part[k, to_y, 0] = (own.astype(jnp.float32) * table).astype(bf16)
            part[k, to_y, 1] = own

        @pl.when(x != k % 2)
        def _():
            x_copy(k).start()

    def pair_sum(k, to_y, i):
        return part[k, to_y, i].astype(jnp.float32) + part_x[k, to_y, i].astype(jnp.float32)

    def pass_chunk(k):
        x_copy(k).wait_recv()
        for i in range(2):
            sum_send[k, i] = pair_sum(k, 1, i).astype(bf16)
        y_copy(k).start()

    def finish_chunk(k):
        y_copy(k).wait_recv()
        numer = pair_sum(k, 0, 0) + sum_recv[k, 0].astype(jnp.float32)
        denom = pair_sum(k, 0, 1) + sum_recv[k, 1].astype(jnp.float32)
        at = pl.multiple_of((k // 2) * piece, BLK)
        out_ref[:, pl.ds(at, piece)] = (numer / denom).astype(bf16)

    load_grads.wait()
    load_scales.wait()
    load_tables.wait()
    greetings = 3 + jnp.where(has_up, 1, 0) + jnp.where(has_down, 1, 0)
    pl.semaphore_wait(barrier, greetings)

    def inside(k):
        return (k >= 0) & (k < chunks)

    def step(s, carry):
        up = s - LAG * z
        down = s - LAG * (layers - 1 - z)

        @pl.when(inside(s - 1))
        def _():
            pool_copy(s - 1).wait_recv()

        @pl.when(inside(up - 1) & has_down)
        def _():
            up_mate(up - 1).wait_recv()

        @pl.when(inside(up - 1) & has_up)
        def _():
            k = up - 1
            up_out[k] = (
                dot(up_pool_sel[...], pooled(k)) + dot(up_in_sel[...], arrived(up_in, k))
            ).astype(bf16)
            up_copy(k).start()

        @pl.when(inside(down - 1) & has_up)
        def _():
            down_mate(down - 1).wait_recv()

        @pl.when(inside(down - 1) & has_down)
        def _():
            k = down - 1
            down_out[k] = (
                dot(down_pool_sel[...], pooled(k)) + dot(down_in_sel[...], arrived(down_in, k))
            ).astype(bf16)
            down_copy(k).start()

        @pl.when(s < chunks)
        def _():
            place(s)
            pool_copy(s).start()

        @pl.when(inside(up) & has_down)
        def _():
            up_copy(up).wait_recv()
            up_mate(up).start()

        @pl.when(inside(down) & has_up)
        def _():
            down_copy(down).wait_recv()
            down_mate(down).start()

        ready = jnp.minimum(up, down) - 1

        @pl.when(inside(ready))
        def _():
            weigh_chunk(ready)

        @pl.when(inside(ready - SETTLE) & (x == (ready - SETTLE) % 2))
        def _():
            pass_chunk(ready - SETTLE)

        @pl.when(inside(ready - 2 * SETTLE) & (x == ready % 2))
        def _():
            finish_chunk(ready - 2 * SETTLE)

        return carry

    lax.fori_loop(0, chunks + 1 + 2 * SETTLE + LAG * (layers - 1), step, 0)

    def drain(k, carry):
        pool_copy(k).wait_send()

        @pl.when(has_up)
        def _():
            up_copy(k).wait_send()
            down_mate(k).wait_send()

        @pl.when(has_down)
        def _():
            down_copy(k).wait_send()
            up_mate(k).wait_send()

        @pl.when(x != k % 2)
        def _():
            x_copy(k).wait_send()

        @pl.when(x == k % 2)
        def _():
            y_copy(k).wait_send()

        return carry

    lax.fori_loop(0, chunks, drain, 0)


def merge_chain(load, collective, token_ids, ids_all, grad_values, grad_scales, tables):
    groups = lax.axis_size("vocab")
    ckpts = lax.axis_size("ckpt")
    rows, width = tables.shape[1:]
    count = token_ids.shape[0]
    capacity = 2 * count // groups
    piece = width // ckpts * 2 // CHAIN_CHUNKS
    chunk_width = 2 * piece
    span = load * capacity // 2
    vmem = pl.BlockSpec(memory_space=pltpu.VMEM)
    hbm = pl.BlockSpec(memory_space=pl.ANY)
    bf16 = jnp.bfloat16
    dma = pltpu.SemaphoreType.DMA
    return pl.pallas_call(
        functools.partial(chain_kernel, groups, ckpts, CHAIN_CHUNKS, span),
        out_shape=jax.ShapeDtypeStruct((rows, width // ckpts), bf16),
        in_specs=[vmem, vmem, hbm, hbm, hbm],
        out_specs=vmem,
        scratch_shapes=[
            pltpu.VMEM((count, width), bf16),
            pltpu.VMEM((rows, width), bf16),
            pltpu.VMEM((width // BLK, count), jnp.float32),
            pltpu.VMEM((count, count), bf16),
            pltpu.VMEM((span, 2 * count), bf16),
            pltpu.VMEM((span, 2 * span), bf16),
            pltpu.VMEM((span, 2 * count), bf16),
            pltpu.VMEM((span, 2 * span), bf16),
            pltpu.VMEM((rows, 2 * count), bf16),
            pltpu.VMEM((rows, 2 * span), bf16),
            pltpu.VMEM((rows, 2 * span), bf16),
            pltpu.VMEM((CHAIN_CHUNKS, 2, count, chunk_width), bf16),
            pltpu.VMEM((CHAIN_CHUNKS, 2, span, chunk_width), bf16),
            pltpu.VMEM((CHAIN_CHUNKS, 2, span, chunk_width), bf16),
            pltpu.VMEM((CHAIN_CHUNKS, span, chunk_width), bf16),
            pltpu.VMEM((CHAIN_CHUNKS, span, chunk_width), bf16),
            pltpu.VMEM((CHAIN_CHUNKS, 2, 2, rows, piece), bf16),
            pltpu.VMEM((CHAIN_CHUNKS, 2, 2, rows, piece), bf16),
            pltpu.VMEM((CHAIN_CHUNKS, 2, rows, piece), bf16),
            pltpu.VMEM((CHAIN_CHUNKS, 2, rows, piece), bf16),
            dma((3,)),
            dma((2, CHAIN_CHUNKS)),
            dma((2, CHAIN_CHUNKS)),
            dma((2, CHAIN_CHUNKS)),
            dma((2, CHAIN_CHUNKS)),
            dma((2, CHAIN_CHUNKS)),
            dma((2, CHAIN_CHUNKS)),
            dma((2, CHAIN_CHUNKS)),
        ],
        compiler_params=pltpu.CompilerParams(
            collective_id=collective, has_side_effects=True, vmem_limit_bytes=60 * 1024 * 1024
        ),
    )(token_ids.reshape(1, count), ids_all, grad_values[0], grad_scales[0], tables[0])


def merge_by_load(token_ids, grad_values, grad_scales, tables):
    groups = lax.axis_size("vocab")
    rows = tables.shape[1]
    count = token_ids.shape[0]
    capacity = 2 * count // groups
    vmem = pl.BlockSpec(memory_space=pltpu.VMEM)
    dma = pltpu.SemaphoreType.DMA
    ids_all, branch = pl.pallas_call(
        functools.partial(gather_kernel, groups, rows, capacity),
        out_shape=[
            jax.ShapeDtypeStruct((groups, count), jnp.int32),
            jax.ShapeDtypeStruct((1,), jnp.int32),
        ],
        in_specs=[vmem],
        out_specs=[vmem, pl.BlockSpec(memory_space=pltpu.SMEM)],
        scratch_shapes=[
            pltpu.VMEM((8, count), jnp.int32),
            pltpu.VMEM((groups, 8, count), jnp.int32),
            dma((groups,)),
            dma((groups,)),
        ],
        compiler_params=pltpu.CompilerParams(collective_id=0, has_side_effects=True),
    )(token_ids.reshape(1, count))
    args = (token_ids, ids_all, grad_values, grad_scales, tables)
    branches = [functools.partial(merge_chain, load, i + 1) for i, load in enumerate(LOADS)]
    branches.append(lambda ids, _, values, scales, rows: merge_rows(ids, values, scales, rows))
    return lax.switch(branch[0], branches, *args)


def merge_small_slots(token_ids, grad_values, grad_scales, tables):
    groups = lax.axis_size("vocab")
    rows = tables.shape[1]
    width = tables.shape[2]
    count = token_ids.shape[0]
    capacity = 2 * count // groups
    owner = token_ids // rows
    same = owner[:, None] == owner[None, :]
    before = lax.broadcasted_iota(jnp.int32, (count, count), 0) < lax.broadcasted_iota(
        jnp.int32, (count, count), 1
    )
    rank = jnp.sum((same & before).astype(jnp.int32), axis=0)
    slot = owner * capacity + rank
    match = lax.broadcasted_iota(jnp.int32, (groups * capacity, count), 0) == slot[None, :]
    scales = grad_scales[0].T
    grads = (
        grad_values[0].astype(jnp.float32).reshape(count, width // BLK, BLK) * scales[:, :, None]
    )
    squares = (grads * grads).reshape(count, width).astype(jnp.bfloat16)
    placed = jnp.dot(match.astype(jnp.bfloat16), squares, preferred_element_type=jnp.float32)
    buffer = placed.astype(jnp.bfloat16).reshape(groups, capacity, width)
    local_rows = token_ids % rows
    row_tags = (
        jnp.sum(jnp.where(match, local_rows[None, :], 0), axis=1)
        .astype(jnp.bfloat16)
        .reshape(groups, capacity)
    )
    arrived, arrived_rows = (
        lax.all_to_all(buffer, "vocab", split_axis=0, concat_axis=0, tiled=True),
        lax.all_to_all(row_tags, "vocab", split_axis=0, concat_axis=0, tiled=True),
    )
    flat_rows = arrived_rows.reshape(groups * capacity).astype(jnp.int32)
    selector = (
        lax.broadcasted_iota(jnp.int32, (rows, groups * capacity), 0) == flat_rows[None, :]
    ).astype(jnp.bfloat16)
    fisher = jnp.dot(
        selector, arrived.reshape(groups * capacity, width), preferred_element_type=jnp.float32
    )
    weight = (fisher + prior_weight).astype(jnp.bfloat16)
    term = (weight.astype(jnp.float32) * tables[0].astype(jnp.float32)).astype(jnp.bfloat16)
    numer, denom = (
        lax.psum_scatter(term, "ckpt", scatter_dimension=1, tiled=True).astype(jnp.float32),
        lax.psum_scatter(weight, "ckpt", scatter_dimension=1, tiled=True).astype(jnp.float32),
    )
    return (numer / denom).astype(jnp.bfloat16)


def per_device(token_ids, grad_values, grad_scales, tables):
    groups = lax.axis_size("vocab")
    ckpts = lax.axis_size("ckpt")
    count = token_ids.shape[0]
    width = tables.shape[2]
    capacity = 2 * count // groups
    if capacity % 16 == 0 and width % (ckpts * CHUNKS * BLK) == 0:
        if groups == 8 and ckpts == 4:
            return merge_by_load(token_ids, grad_values, grad_scales, tables)
        return merge_rows(token_ids, grad_values, grad_scales, tables)
    return merge_small_slots(token_ids, grad_values, grad_scales, tables)


def solution(mesh):
    return jax.shard_map(
        per_device,
        mesh=mesh,
        in_specs=(
            P("vocab"),
            P("ckpt", "vocab", None),
            P("ckpt", None, "vocab"),
            P("ckpt", "vocab", None),
        ),
        out_specs=P("vocab", "ckpt"),
        check_vma=False,
    )
```

profile of v0, /device:TPU:0, one launch (start us, length us, event | category | flops | bytes accessed | tf_op | source)
XLA Modules:
  0.0 106.4 jit_solution(14224904408419673775)
XLA Ops:
  0.0 8.7 %shard_map.52 = (s32[8,128]{1,0:T(8,128)S(1)}, s32[1]{0:T(128)}) custom-call(s32[1,128]{1,0:T(1,128)} %bitcast.44), custom_call_target="tpu_custom_call" | custom-call | tf_op jit(solution)/shard_map/pallas_call | solution.py:775
  9.3 96.3 %conditional.1 = (bf16[128,2048]{1,0:T(8,128)(2,1)S(1)}) conditional(s32[]{:T(128)} %bitcast.25, (s32[128]{0:T(128)}, bf16[1,128,8192]{2,1,0:T(8,128)(2,1)}, f32[1,64,128]{2,1,0:T(8,128)}, bf16[1,128,8192]{2,1,0:T(8,128)(2,1)}, s32[8,128]{1,0:T(8,128)S(1)}) %tuple.23, (s32[128]{0:T(128)}, ...), branch_computations={%region_0.0_spmd, %region_1.0_spmd, %region_2.0_spmd, %region_3.0_... | conditional | flops 1073741824 | bytes 5242888 | solution.py:794
  9.4 95.8 %branch_3_fun.1 = bf16[128,2048]{1,0:T(8,128)(2,1)S(1)} custom-call(s32[1,128]{1,0:T(1,128)} %bitcast.48, s32[8,128]{1,0:T(8,128)S(1)} %get-tuple-element.86.ids_all_ref, bf16[128,8192]{1,0:T(8,128)(2,1)} %bitcast.29, f32[64,128]{1,0:T(8,128)} %bitcast.41, bf16[128,8192]{1,0:T(8,128)(2,1)} %bitcast.35), custom_call_target="tpu_custom_call" | custom-call | tf_op jit(solution)/shard_map/cond/branch_3_fun/pallas_call | solution.py:727
  105.6 0.8 copy.18
where the time goes:
time: 107 us; the launch traced here: 106 us
  Pallas kernels  105 us (98%)
    pallas_call x1, Pallas kernels, merge_chain(): pl.pallas_call(functools.partial(chain_kernel, groups, ckpts, CHAIN_CHUNK...  95.8 us
    pallas_call x1, Pallas kernels, merge_by_load(): pl.pallas_call(functools.partial(gather_kernel, groups, rows, capacity),...  8.73 us

commit v1 on v0

--- a/solution.py
+++ b/solution.py
@@ -12,7 +12,7 @@
 CHAIN_CHUNKS = 32
 LAG = 4
 SETTLE = 2
-LOADS = (8, 9, 10, 11, 12)
+LOADS = (6, 7, 8, 9, 10)
 MESH = pl.DeviceIdType.MESH
 
 
@@ -305,6 +305,23 @@
     return pos_row, pos_col, ids_col[:, 0:1]
 
 
+def meet(a, b):
+    return lax.dot_general(a, b, (((1,), (1,)), ((), ())), preferred_element_type=jnp.float32)
+
+
+def id_counts(ids_all, groups, rows):
+    count = ids_all.shape[1]
+    owners = lax.broadcasted_iota(jnp.int32, (groups, count), 0)
+    locals_ = lax.broadcasted_iota(jnp.int32, (rows, count), 0)
+    counts = []
+    for d in range(groups):
+        ids = ids_all[d : d + 1]
+        by_owner = jnp.where(owners == ids // rows, 1.0, 0.0).astype(jnp.bfloat16)
+        by_row = jnp.where(locals_ == lax.rem(ids, rows), 1.0, 0.0).astype(jnp.bfloat16)
+        counts.append(meet(by_owner, by_row))
+    return counts
+
+
 def gather_kernel(groups, rows, capacity, ids_ref, ids_out, branch_out, mine, theirs, send_sem, recv_sem):
     c = lax.axis_index("ckpt")
     v = lax.axis_index("vocab")
@@ -339,12 +356,14 @@
         copy(j).wait()
     ids_all = jnp.concatenate([theirs[d, 0:1, :] for d in range(groups)], axis=0)
     ids_out[...] = ids_all
-    layer = lax.broadcasted_iota(jnp.int32, (groups, count), 0) // 2
-    owner_layer = ids_all // (2 * rows)
-    most = jnp.zeros((1, 1), jnp.int32)
+    counts = id_counts(ids_all, groups, rows)
+    owner_layer = lax.broadcasted_iota(jnp.int32, (groups, rows), 0) // 2
+    most = jnp.zeros((1, 1), jnp.float32)
     for cut in range(groups // 2 - 1):
-        up = jnp.where((layer <= cut) & (owner_layer > cut), 1, 0)
-        down = jnp.where((layer > cut) & (owner_layer <= cut), 1, 0)
+        below = sum(counts[: 2 * cut + 2])
+        above = sum(counts[2 * cut + 2 :])
+        up = jnp.where((below > 0.0) & (owner_layer > cut), 1.0, 0.0)
+        down = jnp.where((above > 0.0) & (owner_layer <= cut), 1.0, 0.0)
         for flow in (up, down):
             total = jnp.sum(jnp.sum(flow, axis=1, keepdims=True), axis=0, keepdims=True)
             most = jnp.maximum(most, total)
@@ -441,8 +460,11 @@
     match_ref[...] = jnp.where(at0 == pos_row, 1.0, 0.0).astype(bf16)
 
     ids_all = ids_all_ref[...]
-    layer = lax.broadcasted_iota(jnp.int32, (groups, count), 0) // 2
-    owner_layer = ids_all // (2 * rows)
+    counts = id_counts(ids_all, groups, rows)
+    owner_layer = lax.broadcasted_iota(jnp.int32, (groups, rows), 0) // 2
+    named = lax.broadcasted_iota(jnp.int32, (groups, rows), 0) * rows + lax.broadcasted_iota(
+        jnp.int32, (groups, rows), 1
+    )
     before = jnp.where(at0 < at1, 1.0, 0.0).astype(bf16)
 
     def places(mask):
@@ -457,10 +479,16 @@
         place = (inner + jnp.concatenate(offsets, axis=0)).astype(jnp.int32)
         return jnp.where(mask, place, -1)
 
-    up_from = places((layer <= z - 1) & (owner_layer > z - 1))
-    up_to = places((layer <= z) & (owner_layer > z))
-    down_from = places((layer >= z + 1) & (owner_layer < z + 1))
-    down_to = places((layer >= z) & (owner_layer < z))
+    def below(last):
+        return sum(jnp.where(d // 2 <= last, counts[d], 0.0) for d in range(groups)) > 0.0
+
+    def above(first):
+        return sum(jnp.where(d // 2 >= first, counts[d], 0.0) for d in range(groups)) > 0.0
+
+    up_from = places(below(z - 1) & (owner_layer > z - 1))
+    up_to = places(below(z) & (owner_layer > z))
+    down_from = places(above(z + 1) & (owner_layer < z + 1))
+    down_to = places(above(z) & (owner_layer < z))
 
     def one_hot(size, values):
         shape = (size, count)
@@ -468,26 +496,25 @@
             lax.broadcasted_iota(jnp.int32, shape, 0) == values, 1.0, 0.0
         ).astype(bf16)
 
-    def meet(a, b):
-        return lax.dot_general(
-            a, b, (((1,), (1,)), ((), ())), preferred_element_type=jnp.float32
-        )
-
+    tokens = [
+        jnp.broadcast_to(ids_all_ref[pl.ds(2 * z + e, 1), :], (count, count)).T for e in range(2)
+    ]
     up_sum = down_sum = rows_up = rows_down = 0.0
     pools = [[0.0, 0.0] for _ in range(3)]
     for d in range(groups):
         take_up = one_hot(span, up_to[d : d + 1] - core * span)
         take_down = one_hot(span, down_to[d : d + 1] - core * span)
-        take_rows = one_hot(rows, ids_all[d : d + 1] - v * rows)
+        take_rows = one_hot(rows, named[d : d + 1] - v * rows)
         at_up = one_hot(2 * span, up_from[d : d + 1])
         at_down = one_hot(2 * span, down_from[d : d + 1])
         up_sum += meet(take_up, at_up)
         down_sum += meet(take_down, at_down)
         rows_up += meet(take_rows, at_up)
         rows_down += meet(take_rows, at_down)
-        here = jnp.where(z == d // 2, 1.0, 0.0).astype(bf16)
-        for i, take in enumerate((take_up, take_down, take_rows)):
-            pools[i][d % 2] += take * here
+        for e in range(2):
+            at_token = jnp.where(tokens[e] - d * rows == at1, 1.0, 0.0).astype(bf16)
+            for i, take in enumerate((take_up, take_down, take_rows)):
+                pools[i][e] += meet(take, at_token)
     up_in_sel[...] = up_sum.astype(bf16)
     down_in_sel[...] = down_sum.astype(bf16)
     rows_up_sel[...] = rows_up.astype(bf16)
@@ -845,10 +872,10 @@
     groups = lax.axis_size("vocab")
     ckpts = lax.axis_size("ckpt")
     count = token_ids.shape[0]
-    width = tables.shape[2]
+    rows, width = tables.shape[1:]
     capacity = 2 * count // groups
     if capacity % 16 == 0 and width % (ckpts * CHUNKS * BLK) == 0:
-        if groups == 8 and ckpts == 4:
+        if groups == 8 and ckpts == 4 and rows == count:
             return merge_by_load(token_ids, grad_values, grad_scales, tables)
         return merge_rows(token_ids, grad_values, grad_scales, tables)
     return merge_small_slots(token_ids, grad_values, grad_scales, tables)

time: 107 us -> 99.4 us (0.929)
  Pallas kernels: 105 us -> 97.6 us
    pallas_call x1, Pallas kernels: 95.8 us -> 88.6 us  [merge_chain(): pl.pallas_call(functools.partial(chain_kernel, groups, ckpts, CHAIN_CHUNK...]
where the time goes in v1:
time: 99.4 us; the launch traced here: 99.3 us
  Pallas kernels  97.6 us (98%)
    pallas_call x1, Pallas kernels, merge_chain(): pl.pallas_call(functools.partial(chain_kernel, groups, ckpts, CHAIN_CHUNK...  88.6 us
    pallas_call x1, Pallas kernels, merge_by_load(): pl.pallas_call(functools.partial(gather_kernel, groups, rows, capacity),...  8.97 us

profile of v1, /device:TPU:0, one launch (start us, length us, event | category | flops | bytes accessed | tf_op | source)
XLA Modules:
  0.0 99.3 jit_solution(7956886050739371967)
XLA Ops:
  0.0 9.0 %shard_map.52 = (s32[8,128]{1,0:T(8,128)S(1)}, s32[1]{0:T(128)}) custom-call(s32[1,128]{1,0:T(1,128)} %bitcast.44), custom_call_target="tpu_custom_call" | custom-call | tf_op jit(solution)/shard_map/pallas_call | solution.py:802
  9.6 88.9 %conditional.1 = (bf16[128,2048]{1,0:T(8,128)(2,1)S(1)}) conditional(s32[]{:T(128)} %bitcast.25, (s32[128]{0:T(128)}, bf16[1,128,8192]{2,1,0:T(8,128)(2,1)}, f32[1,64,128]{2,1,0:T(8,128)}, bf16[1,128,8192]{2,1,0:T(8,128)(2,1)}, s32[8,128]{1,0:T(8,128)S(1)}) %tuple.23, (s32[128]{0:T(128)}, ...), branch_computations={%region_0.0_spmd, %region_1.0_spmd, %region_2.0_spmd, %region_3.0_... | conditional | flops 1073741824 | bytes 5242888 | solution.py:821
  9.6 88.6 %branch_0_fun.1 = bf16[128,2048]{1,0:T(8,128)(2,1)S(1)} custom-call(s32[1,128]{1,0:T(1,128)} %bitcast.45, s32[8,128]{1,0:T(8,128)S(1)} %get-tuple-element.64.ids_all_ref, bf16[128,8192]{1,0:T(8,128)(2,1)} %bitcast.26, f32[64,128]{1,0:T(8,128)} %bitcast.38, bf16[128,8192]{1,0:T(8,128)(2,1)} %bitcast.32), custom_call_target="tpu_custom_call" | custom-call | tf_op jit(solution)/shard_map/cond/branch_0_fun/pallas_call | solution.py:754
  98.5 0.8 copy.18

commit v2 on v1

--- a/solution.py
+++ b/solution.py
@@ -9,7 +9,7 @@
 
 BLK = 128
 CHUNKS = 16
-CHAIN_CHUNKS = 32
+CHAIN_CHUNKS = 16
 LAG = 4
 SETTLE = 2
 LOADS = (6, 7, 8, 9, 10)

time: 99.4 us -> 96.1 us (0.967)
  Pallas kernels: 97.6 us -> 94.6 us
    pallas_call x1, Pallas kernels: 88.6 us -> 85.6 us  [merge_chain(): pl.pallas_call(functools.partial(chain_kernel, groups, ckpts, CHAIN_CHUNK...]
where the time goes in v2:
time: 96.1 us; the launch traced here: 96.3 us
  Pallas kernels  94.6 us (98%)
    pallas_call x1, Pallas kernels, merge_chain(): pl.pallas_call(functools.partial(chain_kernel, groups, ckpts, CHAIN_CHUNK...  85.6 us
    pallas_call x1, Pallas kernels, merge_by_load(): pl.pallas_call(functools.partial(gather_kernel, groups, rows, capacity),...  8.97 us

profile of v2, /device:TPU:0, one launch (start us, length us, event | category | flops | bytes accessed | tf_op | source)
XLA Modules:
  0.0 96.3 jit_solution(16191208749241282701)
XLA Ops:
  0.0 9.0 %shard_map.52 = (s32[8,128]{1,0:T(8,128)S(1)}, s32[1]{0:T(128)}) custom-call(s32[1,128]{1,0:T(1,128)} %bitcast.44), custom_call_target="tpu_custom_call" | custom-call | tf_op jit(solution)/shard_map/pallas_call | solution.py:802
  9.6 85.9 %conditional.1 = (bf16[128,2048]{1,0:T(8,128)(2,1)S(1)}) conditional(s32[]{:T(128)} %bitcast.25, (s32[128]{0:T(128)}, bf16[1,128,8192]{2,1,0:T(8,128)(2,1)}, f32[1,64,128]{2,1,0:T(8,128)}, bf16[1,128,8192]{2,1,0:T(8,128)(2,1)}, s32[8,128]{1,0:T(8,128)S(1)}) %tuple.23, (s32[128]{0:T(128)}, ...), branch_computations={%region_0.0_spmd, %region_1.0_spmd, %region_2.0_spmd, %region_3.0_... | conditional | flops 1073741824 | bytes 5242888 | solution.py:821
  9.6 85.6 %branch_2_fun.1 = bf16[128,2048]{1,0:T(8,128)(2,1)S(1)} custom-call(s32[1,128]{1,0:T(1,128)} %bitcast.47, s32[8,128]{1,0:T(8,128)S(1)} %get-tuple-element.81.ids_all_ref, bf16[128,8192]{1,0:T(8,128)(2,1)} %bitcast.28, f32[64,128]{1,0:T(8,128)} %bitcast.40, bf16[128,8192]{1,0:T(8,128)(2,1)} %bitcast.34), custom_call_target="tpu_custom_call" | custom-call | tf_op jit(solution)/shard_map/cond/branch_2_fun/pallas_call | solution.py:754
  95.5 0.8 copy.18
